TPU v7x, 128 devices: a whole 4x4x4 slice. The times are simulated.
128 devices in a mesh: section: 8 (over y_lo, x), expert: 16 (over y_hi, z, core).
Axes of the slice: x: 4, y: 4 (y_hi: 2, y_lo: 2; y = y_hi * 2 + y_lo), z: 4, core: 2. Of those that a mesh axis runs over, the one named last changes fastest.
Arguments:
- tokens: bfloat16 [2, 8, 1024, 7168], P(None, 'section', 'expert'), may hold values from -6 to 6
- route_ids: int32 [2, 8, 1024, 2], P(None, 'section', 'expert'), may hold values from 0 to 3, as said below
- slot_index: int32 [2, 8, 1024, 2], P(None, 'section', 'expert'), may hold values from 0 to 32, as said below
- gate_values: float32 [2, 8, 1024, 2], P(None, 'section', 'expert'), may hold values from 0.2 to 1
- w_gate: bfloat16 [8, 16, 7168, 512], P('section', 'expert'), may hold values from -0.0625 to 0.0625
- w_up: bfloat16 [8, 16, 7168, 512], P('section', 'expert'), may hold values from -0.0625 to 0.0625
- w_down: bfloat16 [8, 16, 512, 7168], P('section', 'expert'), may hold values from -0.125 to 0.125
Outputs:
- handed: bfloat16 [2, 8, 1024, 7168], P(None, 'section', 'expert')
Inputs may be any that keep to these rules, and one draw needn't show every extreme that they name: `route_ids`: each row names 2 different experts. `slot_index`: within the rows of one device of one front and layer, the choices naming one expert are numbered 0, 1, 2, ... in some order; numbers from 32 on are replaced by 32, which marks a dropped choice.
All inputs are finite; a program needn't handle non-finite values.
Results may differ from a plain program's by a relative error of at most 0.015.
Values may be sent and summed in bfloat16 or wider, within the bound.
A program may use at most 256 MiB of HBM per device.

v0:
```python
import jax
import jax.numpy as jnp
from jax import lax
from jax.sharding import PartitionSpec as P

D = 7168
TILE = 128
WSPLIT = 4


def shifted(block, axis, distance):
    devices = range(lax.axis_size(axis))
    route = [((i - distance) % len(devices), i) for i in devices]
    return lax.ppermute(block, axis, route)


def coarse_grid(values):
    magnitude = jnp.abs(values)
    spacing = jnp.full_like(magnitude, 2.0 ** (-9))
    for power in range(-5, 9):
        spacing = jnp.where(magnitude >= 2.0**power, 2.0 ** (power - 3), spacing)
    snapped = jnp.minimum(jnp.floor(magnitude / spacing + 0.5) * spacing, 448.0)
    return jnp.where(values < 0, -snapped, snapped)


def expert_rows(coded_in, scale_in, weight_gate, weight_up, weight_down):
    shape = coded_in.shape
    restored = (
        coded_in.astype(jnp.float32).reshape(shape[:-1] + (D // TILE, TILE)) * scale_in[..., None]
    )
    rows = restored.reshape(-1, D).astype(jnp.bfloat16)
    gate = jnp.dot(rows, weight_gate, preferred_element_type=jnp.float32)
    up = jnp.dot(rows, weight_up, preferred_element_type=jnp.float32)
    hidden = (jax.nn.silu(gate) * up).astype(jnp.bfloat16)
    part = jnp.dot(hidden, weight_down, preferred_element_type=jnp.float32).astype(jnp.bfloat16)
    return part.reshape(shape)


def local(tokens, route_ids, slot_index, gate_values, w_gate, w_up, w_down):
    n_dev = lax.axis_size("expert")
    nexp = n_dev // WSPLIT
    x_rows = tokens[:, 0].astype(jnp.float32)
    tok = x_rows.shape[1]
    slots_cap = tok // 2
    ids = route_ids[:, 0]
    slots = slot_index[:, 0]
    gates = gate_values[:, 0]
    weight_gate = w_gate[0, 0]
    weight_up = w_up[0, 0]
    weight_down = w_down[0, 0]
    tiles = x_rows.reshape(2, tok, D // TILE, TILE)
    scale = (jnp.max(jnp.abs(tiles), axis=-1) + 1e-06) / 448.0
    coded = coarse_grid(tiles / scale[..., None]).astype(jnp.bfloat16).reshape(2, tok, D)
    ehot = (ids[..., None] == jnp.arange(nexp, dtype=jnp.int32)).astype(jnp.float32)
    chot = (slots[..., None] == jnp.arange(slots_cap, dtype=jnp.int32)).astype(jnp.float32)
    select = jnp.einsum("ftke,ftkc->fect", ehot, chot).astype(jnp.bfloat16)
    sent = jnp.einsum("fect,ftd->fecd", select, coded, preferred_element_type=jnp.float32).astype(
        jnp.bfloat16
    )
    sent_scale = jnp.einsum(
        "fect,ftd->fecd", select.astype(jnp.float32), scale, precision=lax.Precision.HIGHEST
    )
    sent = jnp.broadcast_to(sent[:, :, None], (2, nexp, WSPLIT, slots_cap, D)).reshape(
        2, n_dev, slots_cap, D
    )
    sent_scale = jnp.broadcast_to(sent_scale[:, :, None], (2, nexp, WSPLIT, slots_cap, D // TILE))
    sent_scale = sent_scale.reshape(2, n_dev, slots_cap, D // TILE)
    arrived = expert_rows(
        lax.all_to_all(sent, "expert", split_axis=1, concat_axis=1, tiled=True),
        lax.all_to_all(
            sent_scale.astype(jnp.bfloat16), "expert", split_axis=1, concat_axis=1, tiled=True
        ).astype(sent_scale.dtype),
        weight_gate,
        weight_up,
        weight_down,
    )
    returned = lax.all_to_all(arrived, "expert", split_axis=1, concat_axis=1, tiled=True)
    expert_out = jnp.sum(
        returned.astype(jnp.float32).reshape(2, nexp, WSPLIT, slots_cap, D), axis=2
    )
    weights = jnp.einsum("ftke,ftkc,ftk->fect", ehot, chot, gates)
    branch = jnp.einsum("fect,fecd->ftd", weights, expert_out, precision=lax.Precision.HIGHEST)
    layer_out = (x_rows + branch).astype(jnp.bfloat16)
    upward = shifted(layer_out[0:1], "section", 1)
    downward = shifted(layer_out[1:2], "section", -1)
    return jnp.concatenate([upward, downward], axis=0)[:, None]


def solution(mesh):
    placed = (
        P(None, "section", "expert", None),
        P(None, "section", "expert", None),
        P(None, "section", "expert", None),
        P(None, "section", "expert", None),
        P("section", "expert", None, None),
        P("section", "expert", None, None),
        P("section", "expert", None, None),
    )
    return jax.shard_map(
        local,
        mesh=mesh,
        in_specs=placed,
        out_specs=P(None, "section", "expert", None),
        check_vma=False,
    )
```

profile of v0, /device:TPU:0, one launch (start us, length us, event | category | flops | bytes accessed | tf_op | source)
XLA Modules:
  0.0 595.3 jit_solution(7799748048546874381)
XLA Ops:
  0.0 0.8 copy.42
  0.8 0.8 copy.44
  1.6 0.9 fusion.14
  2.5 0.1 copy.45
  2.6 1.9 convert_abs_fusion
  4.5 0.6 copy.61
  5.1 1.0 bitcast_reduce_fusion
  6.1 0.2 convolution_convert_fusion.3
  6.4 1.1 reshape.50
  7.5 8.1 %all-to-all-start.1 = ((bf16[16,2,1792]{2,1,0:T(2,128)(2,1)}), bf16[16,2,1792]{2,1,0:T(2,128)(2,1)S(1)}, u32[]{:S(2)}, u32[]{:S(2)}) async-start(bf16[16,2,1792]{2,1,0:T(2,128)(2,1)} %reshape.50), calls=%async_computation.1 | async-start | bytes 229376 | tf_op jit(solution)/shard_map/all_to_all | solution.py:70
  15.7 2.4 div.27
  18.0 0.0 copy-start
  18.0 5.0 div.28
  23.0 0.0 copy-done
  23.0 7.2 %convolution_convert_fusion.1 = bf16[2,4,32,7168]{3,2,1,0:T(8,128)(2,1)S(1)} fusion(bf16[2,4,32,64]{3,2,1,0:T(8,128)(2,1)S(1)} %copy.45, f32[2,64,7168]{2,1,0:T(8,128)} %div.28, bf16[2,1,64,7168]{3,2,1,0:T(8,128)(2,1)S(1)} %copy-done), kind=kOutput, calls=%fused_computation.3 | convolution fusion | flops 273416192 | bytes 9207808 | tf_op jit(solution)/shard_map/fect,ftd->fecd/dot_general | solution.py:57
  30.2 2.0 copy.46
  32.2 0.0 all-to-all-done.1
  32.2 6.6 %broadcast_in_dim.80 = bf16[2,4,4,32,7168]{4,3,0,2,1:T(8,128)(2,1)} broadcast(bf16[2,4,32,7168]{3,2,0,1:T(8,128)(2,1)} %copy.46), dimensions={0,1,3,4} | broadcast | bytes 18350080 | tf_op jit(solution)/shard_map/broadcast_in_dim | solution.py:63
  38.9 7.3 %all-to-all-start = ((bf16[2,16,32,7168]{3,2,0,1:T(8,128)(2,1)}), bf16[2,16,32,7168]{3,2,0,1:T(8,128)(2,1)}, u32[]{:S(2)}, u32[]{:S(2)}) async-start(bf16[2,16,32,7168]{3,2,0,1:T(8,128)(2,1)} %bitcast.83), calls=%async_computation | async-start | bytes 29360128 | tf_op jit(solution)/shard_map/all_to_all | solution.py:69
  46.2 0.4 reshape.51
  46.6 0.1 copy.51
  46.7 10.1 %mul.25 = f32[2,16,32,56,128]{4,3,2,1,0:T(8,128)} broadcast(f32[2,16,32,56]{3,2,1,0:T(8,128)S(1)} %copy.51), dimensions={0,1,2,3} | broadcast | bytes 29589504 | tf_op jit(solution)/shard_map/mul | solution.py:29
  56.8 30.5 %mul.26 = f32[2,16,32,7168]{3,2,1,0:T(8,128)} reshape(f32[2,16,32,56,128]{4,3,2,1,0:T(8,128)} %mul.25) | data formatting | bytes 58720256 | tf_op jit(solution)/shard_map/mul | solution.py:29
  87.3 180.0 %all-to-all-done = bf16[2,16,32,7168]{3,2,0,1:T(8,128)(2,1)} async-done(((bf16[2,16,32,7168]{3,2,0,1:T(8,128)(2,1)}), bf16[2,16,32,7168]{3,2,0,1:T(8,128)(2,1)}, u32[]{:S(2)}, u32[]{:S(2)}) %all-to-all-start) | async-done | bytes 14680096 | tf_op jit(solution)/shard_map/all_to_all | solution.py:69
  267.3 0.0 slice-start
  267.3 15.4 %multiply_convert_fusion = bf16[2,16,32,7168]{3,2,1,0:T(8,128)(2,1)S(1)} fusion(f32[2,16,32,7168]{3,2,1,0:T(8,128)} %mul.26, bf16[2,16,32,7168]{3,2,0,1:T(8,128)(2,1)} %all-to-all-done), kind=kLoop, calls=%fused_computation.1 | loop fusion | flops 22020096 | bytes 58720256 | tf_op jit(solution)/shard_map/convert_element_type | solution.py:31
  282.7 0.0 slice-start.1
  282.7 10.3 %fusion.3 = f32[1024,512]{1,0:T(8,128)S(1)} fusion(bf16[1024,7168]{1,0:T(8,128)(2,1)S(1)} %bitcast.84, bf16[1,1,7168,512]{3,2,1,0:T(8,128)(2,1)} %param.12), kind=kOutput, calls=%fused_computation.8 | convolution fusion | flops 7516192768 | bytes 24117248 | tf_op jit(solution)/shard_map/dot_general | solution.py:33
  293.0 0.0 slice-done
  293.0 0.0 slice-done.1
  293.1 9.0 %multiply_convert_fusion.1 = bf16[1024,512]{1,0:T(8,128)(2,1)} fusion(f32[1024,512]{1,0:T(8,128)S(1)} %fusion.3, bf16[1024,7168]{1,0:T(8,128)(2,1)S(1)} %bitcast.85, bf16[1,1,7168,512]{3,2,1,0:T(8,128)(2,1)S(1)} %bitcast.95), kind=kOutput, calls=%fused_computation.19 | convolution fusion | flops 7519338496 | bytes 25165824 | tf_op jit(solution)/shard_map/dot_general | solution.py:32
  302.1 10.3 %convolution_convert_fusion = bf16[1024,7168]{1,0:T(8,128)(2,1)S(1)} fusion(bf16[1024,512]{1,0:T(8,128)(2,1)} %multiply_convert_fusion.1, bf16[1,1,512,7168]{3,2,1,0:T(8,128)(2,1)} %param.13), kind=kOutput, calls=%fused_computation.2 | convolution fusion | flops 7523532800 | bytes 23068672 | tf_op jit(solution)/shard_map/dot_general | solution.py:35
  312.4 6.3 %copy.52 = bf16[2,16,32,7168]{3,2,0,1:T(8,128)(2,1)} copy(bf16[2,16,32,7168]{3,2,1,0:T(8,128)(2,1)S(1)} %bitcast.86) | data formatting | bytes 29360128 | tf_op jit(solution)/shard_map/reshape | solution.py:36
  318.7 0.0 copy-start.1
  318.7 13.7 %all-to-all-start.2 = ((bf16[2,16,32,7168]{3,2,0,1:T(8,128)(2,1)}), bf16[2,16,32,7168]{3,2,0,1:T(8,128)(2,1)}, u32[]{:S(2)}, u32[]{:S(2)}) async-start(bf16[2,16,32,7168]{3,2,0,1:T(8,128)(2,1)} %copy.52), calls=%async_computation.2 | async-start | bytes 29360128 | tf_op jit(solution)/shard_map/all_to_all | solution.py:77
  332.4 0.0 copy-done.1
  332.4 0.1 copy.43
  332.5 1.0 convolution_bitcast_fusion.1
  333.5 220.0 %all-to-all-done.2 = bf16[2,16,32,7168]{3,2,0,1:T(8,128)(2,1)} async-done(((bf16[2,16,32,7168]{3,2,0,1:T(8,128)(2,1)}), bf16[2,16,32,7168]{3,2,0,1:T(8,128)(2,1)}, u32[]{:S(2)}, u32[]{:S(2)}) %all-to-all-start.2) | async-done | bytes 14680096 | tf_op jit(solution)/shard_map/all_to_all | solution.py:77
  553.5 8.8 %convert_reduce_fusion = f32[2,4,32,7168]{3,2,0,1:T(8,128)S(1)} fusion(bf16[2,16,32,7168]{3,2,0,1:T(8,128)(2,1)} %all-to-all-done.2), kind=kLoop, calls=%fused_computation | loop fusion | flops 12845056 | bytes 22020096 | tf_op jit(solution)/shard_map/reduce_sum | solution.py:78
  562.4 7.2 %fusion.1 = bf16[2,64,7168]{2,1,0:T(8,128)(2,1)S(1)} fusion(f32[2,4,32,7168]{3,2,0,1:T(8,128)S(1)} %convert_reduce_fusion, bf16[2,1,64,7168]{3,2,1,0:T(8,128)(2,1)S(1)} %copy-done, f32[2,4,32,64]{2,1,3,0:T(4,128)S(1)} %convolution_bitcast_fusion.1), kind=kOutput, calls=%fused_computation.6 | convolution fusion | flops 1412038656 | bytes 11075584 | tf_op jit(solution)/shard_map/fect,fecd->ftd/dot_general | solution.py:82
  569.6 0.1 fusion.45
  569.7 1.6 collective-permute-start
  571.3 2.6 collective-permute-start.1
  573.9 19.9 %collective-permute-done = bf16[1,64,7168]{2,1,0:T(8,128)(2,1)S(1)} collective-permute-done((bf16[1,64,7168]{2,1,0:T(8,128)(2,1)S(1)}, bf16[1,64,7168]{2,1,0:T(8,128)(2,1)S(1)}, u32[]{:S(2)}, u32[]{:S(2)}) %collective-permute-start) | collective-permute-done | bytes 917536 | tf_op jit(solution)/shard_map/ppermute | solution.py:14
  593.9 0.0 collective-permute-done.1
  593.9 1.4 maximum_bitcast_fusion
  (4 shorter events, 0.1 us)
Async XLA Ops:
  7.5 24.7 %all-to-all-start.1 = ((bf16[16,2,1792]{2,1,0:T(2,128)(2,1)}), bf16[16,2,1792]{2,1,0:T(2,128)(2,1)S(1)}, u32[]{:S(2)}, u32[]{:S(2)}) async-start(bf16[16,2,1792]{2,1,0:T(2,128)(2,1)} %reshape.50), calls=%async_computation.1 | async-start | bytes 229376 | tf_op jit(solution)/shard_map/all_to_all | solution.py:70
  18.0 5.0 copy-start
  38.9 228.4 %all-to-all-start = ((bf16[2,16,32,7168]{3,2,0,1:T(8,128)(2,1)}), bf16[2,16,32,7168]{3,2,0,1:T(8,128)(2,1)}, u32[]{:S(2)}, u32[]{:S(2)}) async-start(bf16[2,16,32,7168]{3,2,0,1:T(8,128)(2,1)} %bitcast.83), calls=%async_computation | async-start | bytes 29360128 | tf_op jit(solution)/shard_map/all_to_all | solution.py:69
  267.3 25.8 %slice-start = ((s8[7340032]{0:T(1024)(128)(4,1)}), s8[4194304]{0:T(1024)(128)(4,1)S(1)}, s32[]{:S(2)}) async-start(s8[7340032]{0:T(1024)(128)(4,1)} %bitcast.94), calls=%async_computation.3 | async-start | bytes 8388608
  282.7 10.3 %slice-start.1 = ((s8[7340032]{0:T(1024)(128)(4,1)}), s8[3145728]{0:T(1024)(128)(4,1)S(1)}, s32[]{:S(2)}) async-start(s8[7340032]{0:T(1024)(128)(4,1)} %bitcast.94), calls=%async_computation.4 | async-start | bytes 6291456
  318.7 13.7 %copy-start.1 = (f32[2,1,64,2]{2,3,1,0:T(2,128)S(1)}, f32[2,1,64,2]{2,3,1,0:T(2,128)}, u32[]{:S(2)}) copy-start(f32[2,1,64,2]{2,3,1,0:T(2,128)} %param.10) | copy-start | bytes 3076
  318.7 234.9 %all-to-all-start.2 = ((bf16[2,16,32,7168]{3,2,0,1:T(8,128)(2,1)}), bf16[2,16,32,7168]{3,2,0,1:T(8,128)(2,1)}, u32[]{:S(2)}, u32[]{:S(2)}) async-start(bf16[2,16,32,7168]{3,2,0,1:T(8,128)(2,1)} %copy.52), calls=%async_computation.2 | async-start | bytes 29360128 | tf_op jit(solution)/shard_map/all_to_all | solution.py:77
  569.7 24.1 %collective-permute-start = (bf16[1,64,7168]{2,1,0:T(8,128)(2,1)S(1)}, bf16[1,64,7168]{2,1,0:T(8,128)(2,1)S(1)}, u32[]{:S(2)}, u32[]{:S(2)}) collective-permute-start(bf16[1,64,7168]{2,1,0:T(8,128)(2,1)S(1)} %get-tuple-element.5), channel_id=1, source_target_pairs={{112,0},{0,16},{16,32},{32,48},{48,64},{64,80},{80,96},{96,112},{1... | collective-permute-start | bytes 2752520 | tf_op jit(solution)/shard_map/ppermute | solution.py:14
  571.3 22.6 %collective-permute-start.1 = (bf16[1,64,7168]{2,1,0:T(8,128)(2,1)S(1)}, bf16[1,64,7168]{2,1,0:T(8,128)(2,1)S(1)}, u32[]{:S(2)}, u32[]{:S(2)}) collective-permute-start(bf16[1,64,7168]{2,1,0:T(8,128)(2,1)S(1)} %get-tuple-element.6), channel_id=1, source_target_pairs={{16,0},{32,16},{48,32},{64,48},{80,64},{96,80},{112,96},{0,112},{1... | collective-permute-start | bytes 2752520 | tf_op jit(solution)/shard_map/ppermute | solution.py:14
where the time goes:
time: 603 us; the launch traced here: 595 us
  waiting for transfers between devices  420 us (70%)
  local copies, waits for them, and re-layouts  67.1 us (11%)
  matrix products  46.1 us (8%)
  starting transfers between devices  33.3 us (6%)
  other arithmetic  28.6 us (5%)
    all_to_all x1, waiting for transfers between devices, local(): lax.all_to_all(arrived, 'expert', split_axis=1, concat_axis=1, tiled=True)  220 us
    all_to_all x1, waiting for transfers between devices, local(): lax.all_to_all(sent, 'expert', split_axis=1, concat_axis=1, tiled=True)  180 us
    mul x2, local copies, waits for them, and re-layouts, expert_rows(): coded_in.astype(jnp.float32).reshape(shape[:-1] + (D // TILE, TILE))  40.6 us
    ppermute x2, waiting for transfers between devices, shifted(): return lax.ppermute(block, axis, route)  19.9 us
    convert_element_type x1, other arithmetic, expert_rows(): rows = restored.reshape(-1, D).astype(jnp.bfloat16)  15.4 us
    all_to_all x1, starting transfers between devices, local(): lax.all_to_all(arrived, 'expert', split_axis=1, concat_axis=1, tiled=True)  13.7 us
  transfers between devices with their start and end apart: 5, of which 3 were waited for; matrix products, arithmetic and copies ran while one was open for 10% of the time, Pallas kernels for 0%

commit v1 on v0

v1 whole, which is shorter than its diff:
```python
import jax
import jax.numpy as jnp
from jax import lax
from jax.experimental import pallas as pl
from jax.experimental.pallas import tpu as pltpu
from jax.sharding import PartitionSpec as P

D = 7168
TILE = 128
TOK = 64
CAP = 32
H = 512
CW = 1024
NC = D // CW
HC = 256
KC = 1024
MESH = pl.DeviceIdType.MESH

CORE = 1
PAIR = 2
CROSS = 6
FAR = 8
DIAG = 14
PARTNERS = (CORE, PAIR, CROSS, FAR, DIAG)

BF = jnp.bfloat16
F32 = jnp.float32


def snap(values):
    mag = jnp.abs(values)
    spacing = jnp.full_like(mag, 2.0**-9)
    for power in range(-5, 9):
        spacing = jnp.where(mag >= 2.0**power, 2.0 ** (power - 3), spacing)
    inverse = jnp.full_like(mag, 2.0**9)
    for power in range(-5, 9):
        inverse = jnp.where(mag >= 2.0**power, 2.0 ** (3 - power), inverse)
    snapped = jnp.minimum(jnp.floor(mag * inverse + 0.5) * spacing, 448.0)
    return jnp.where(values < 0, -snapped, snapped)


def kernel(
    tok_hbm, meta, wg, wu, wd, out, wg2, wu2, wd2,
    tokv, rest, rest_p, meta_p,
    xrows, s_x, s_y, s_d,
    wbuf, dbuf, hid,
    loc, g_x, g_y, g_p, keep, g_d, g_t,
    r_x, r_y, r_p, r_d, r_t, fin,
    tok_sem, w_sem, d_sem, wx_s, wx_r, meta_s, meta_r,
    dis_s, dis_r, com_s, com_r, h_s, h_r,
):
    me = lax.axis_index("expert")
    sec = lax.axis_index("section")
    n_sec = lax.axis_size("section")
    up = lax.rem(sec + 1, n_sec)
    down = lax.rem(sec + n_sec - 1, n_sec)
    mine = (me // 8) * 2 + (me // 4) % 2

    def remote(src, dst, ss, rs, mask):
        return pltpu.make_async_remote_copy(
            src_ref=src, dst_ref=dst, send_sem=ss, recv_sem=rs,
            device_id=(sec, me ^ mask), device_id_type=MESH,
        )

    def tok_copy(f):
        return pltpu.make_async_copy(tok_hbm.at[f], tokv.at[f], tok_sem.at[f])

    def w_copies(ci):
        gate_src, up_src = ((wg, wu), (wg2, wu2))[ci // 2]
        cols = pl.ds((ci % 2) * HC, HC)
        slot = ci % 2
        return (
            pltpu.make_async_copy(gate_src.at[:, cols], wbuf.at[slot, 0], w_sem.at[slot, 0]),
            pltpu.make_async_copy(up_src.at[:, cols], wbuf.at[slot, 1], w_sem.at[slot, 1]),
        )

    def d_copies(j):
        slot = lax.rem(j, 2)
        cols = pl.ds(pl.multiple_of(j * CW, CW), CW)
        return (
            pltpu.make_async_copy(wd.at[:, cols], dbuf.at[slot, pl.ds(0, H)], d_sem.at[slot, 0]),
            pltpu.make_async_copy(wd2.at[:, cols], dbuf.at[slot, pl.ds(H, H)], d_sem.at[slot, 1]),
        )

    for f in range(2):
        tok_copy(f).start()
    for cp in w_copies(0):
        cp.start()

    barrier = pltpu.get_barrier_semaphore()
    for mask in PARTNERS:
        pl.semaphore_signal(barrier, inc=1, device_id=(sec, me ^ mask), device_id_type=MESH)
    for other in (up, down):
        pl.semaphore_signal(barrier, inc=1, device_id=(other, me), device_id_type=MESH)
    pl.semaphore_wait(barrier, len(PARTNERS) + 2)

    w_moves = [
        remote(src, dst, wx_s.at[i], wx_r.at[i], CORE)
        for i, (src, dst) in enumerate(((wg, wg2), (wu, wu2), (wd, wd2)))
    ]
    meta_move = remote(meta, meta_p, meta_s, meta_r, PAIR)
    meta_move.start()

    def restore(f):
        tok_copy(f).wait()

        def step(i, carry):
            for k in range(4):
                cols = pl.ds(pl.multiple_of(i * (4 * TILE), 4 * TILE) + k * TILE, TILE)
                t = tokv[f, :, cols].astype(F32)
                scale = (jnp.max(jnp.abs(t), axis=-1, keepdims=True) + 1e-6) / 448.0
                rest[f, :, cols] = (snap(t * (1.0 / scale)) * scale).astype(BF)
            return carry

        lax.fori_loop(0, D // (4 * TILE), step, 0)

    def selection(table, f, rows):
        row = lax.broadcasted_iota(jnp.int32, (rows, TOK), 0)
        code = ((mine ^ (row // CAP)) * (CAP + 1) + row % CAP).astype(F32)
        hit = (table[f, TOK : TOK + 1, :TOK] == code) | (table[f, TOK + 1 : TOK + 2, :TOK] == code)
        return jnp.where(hit, 1.0, 0.0).astype(BF)

    def gating(table, f, cols):
        col = lax.broadcasted_iota(jnp.int32, (TOK, cols), 1)
        code = ((mine ^ (col // CAP)) * (CAP + 1) + col % CAP).astype(F32)
        weight = jnp.where(table[f, :TOK, 0:1] == code, table[f, :TOK, 2:3], 0.0)
        weight = weight + jnp.where(table[f, :TOK, 1:2] == code, table[f, :TOK, 3:4], 0.0)
        high = weight.astype(BF)
        return high, (weight - high.astype(F32)).astype(BF)

    def pick(f, sel, source, targets):
        def step(j, carry):
            cols = pl.ds(pl.multiple_of(j * CW, CW), CW)
            got = jnp.dot(sel, source[f, :, cols], preferred_element_type=F32).astype(BF)
            for i, (ref, first) in enumerate(targets):
                ref[f, first : first + CAP, cols] = got[i * CAP : (i + 1) * CAP]
            return carry

        lax.fori_loop(0, NC, step, 0)

    def dispatch(f, i):
        row = lambda b: pl.ds(b * CAP, CAP)
        src, dst, mask = (
            (rest.at[f], rest_p.at[f], PAIR),
            (s_d.at[f], xrows.at[f, row(6)], DIAG),
            (s_y.at[f, row(0)], xrows.at[f, row(4)], FAR),
            (s_x.at[f, row(0)], xrows.at[f, row(2)], CROSS),
            (s_y.at[f, row(1)], xrows.at[f, row(5)], FAR),
            (s_x.at[f, row(1)], xrows.at[f, row(3)], CROSS),
            (xrows.at[f, row(6)], xrows.at[f, row(7)], PAIR),
        )[i]
        return remote(src, dst, dis_s.at[f, i], dis_r.at[f, i], mask)

    def prepare(f):
        restore(f)

    def send_own(f):
        dispatch(f, 0).start()
        pick(f, selection(meta, f, 4 * CAP), rest, ((xrows, 0), (s_x, 0), (s_y, 0), (s_d, 0)))
        for i in (1, 2, 3):
            dispatch(f, i).start()

    def send_partner(f):
        dispatch(f, 0).wait_recv()
        pick(f, selection(meta_p, f, 3 * CAP), rest_p, ((xrows, CAP), (s_x, CAP), (s_y, CAP)))
        dispatch(f, 4).start()
        dispatch(f, 5).start()
        dispatch(f, 1).wait_recv()
        dispatch(f, 6).start()

    def gate_up(f):
        for ci in range(4):
            for cp in w_copies(ci):
                cp.wait()
            if ci == 1 and f == 0:
                w_moves[0].wait_recv()
                w_moves[1].wait_recv()
            if ci < 3:
                for cp in w_copies(ci + 1):
                    cp.start()
            elif f == 0:
                for cp in w_copies(0):
                    cp.start()

            def step(k, acc):
                rows = pl.ds(pl.multiple_of(k * KC, KC), KC)
                x = xrows[f, :, rows]
                g = jnp.dot(x, wbuf[ci % 2, 0, rows, :], preferred_element_type=F32)
                u = jnp.dot(x, wbuf[ci % 2, 1, rows, :], preferred_element_type=F32)
                return acc[0] + g, acc[1] + u

            zero = jnp.zeros((8 * CAP, HC), F32)
            g, u = lax.fori_loop(0, D // KC, step, (zero, zero))
            hid[f, :, ci * HC : (ci + 1) * HC] = (g / (1.0 + jnp.exp(-g)) * u).astype(BF)

    def combine(f, j, i):
        src, dst, mask = (
            (g_p, r_p, PAIR),
            (g_x, r_x, CROSS),
            (g_y, r_y, FAR),
            (g_d, r_d, DIAG),
            (g_t, r_t, PAIR),
        )[i]
        return remote(src.at[f, j], dst.at[f, j], com_s.at[f, j, i], com_r.at[f, j, i], mask)

    def first(f, j):
        for cp in d_copies(j):
            cp.wait()

        @pl.when(j < NC - 1)
        def _():
            for cp in d_copies(j + 1):
                cp.start()

        q = jnp.dot(hid[f], dbuf[lax.rem(j, 2)], preferred_element_type=F32).astype(BF)
        g_p[f, j] = q[7 * CAP :]
        g_x[f, j] = q[2 * CAP : 4 * CAP]
        g_y[f, j] = q[4 * CAP : 6 * CAP]
        for i in range(3):
            combine(f, j, i).start()
        loc[f, j] = q[: 2 * CAP]
        keep[f, j] = q[6 * CAP : 7 * CAP]

    def gated(weights, parts):
        z = jnp.concatenate(parts, axis=0)
        high, low = weights
        return jnp.dot(high, z, preferred_element_type=F32) + jnp.dot(low, z, preferred_element_type=F32)

    def second(f, j, weights):
        combine(f, j, 0).wait_recv()
        g_d[f, j] = (keep[f, j].astype(F32) + r_p[f, j].astype(F32)).astype(BF)
        combine(f, j, 3).start()
        combine(f, j, 1).wait_recv()
        combine(f, j, 2).wait_recv()
        g_t[f, j] = gated(weights, [loc[f, j, CAP:], r_x[f, j, CAP:], r_y[f, j, CAP:]]).astype(BF)
        combine(f, j, 4).start()

    def handoff(f, j):
        cols = pl.ds(pl.multiple_of(j * CW, CW), CW)
        return pltpu.make_async_remote_copy(
            src_ref=fin.at[f, j], dst_ref=out.at[f, :, cols],
            send_sem=h_s.at[f, j], recv_sem=h_r.at[f, j],
            device_id=((up, down)[f], me), device_id_type=MESH,
        )

    def third(f, j, weights):
        cols = pl.ds(pl.multiple_of(j * CW, CW), CW)
        combine(f, j, 3).wait_recv()
        combine(f, j, 4).wait_recv()
        total = gated(weights, [loc[f, j, :CAP], r_x[f, j, :CAP], r_y[f, j, :CAP], r_d[f, j]])
        total = total + r_t[f, j].astype(F32) + tokv[f, :, cols].astype(F32)
        fin[f, j] = total.astype(BF)
        handoff(f, j).start()

    def loop(body):
        def step(j, carry):
            body(j)
            return carry

        lax.fori_loop(0, NC, step, 0)

    prepare(0)
    send_own(0)
    for move in w_moves:
        move.start()
    prepare(1)
    meta_move.wait_recv()
    send_partner(0)
    send_own(1)
    for i in (2, 3, 4, 5, 6):
        dispatch(0, i).wait_recv()
    gate_up(0)
    w_moves[2].wait_recv()
    for cp in d_copies(0):
        cp.start()
    send_partner(1)
    loop(lambda j: first(0, j))
    for i in (2, 3, 4, 5, 6):
        dispatch(1, i).wait_recv()
    gate_up(1)
    for cp in d_copies(0):
        cp.start()
    theirs0 = gating(meta_p, 0, 3 * CAP)
    theirs1 = gating(meta_p, 1, 3 * CAP)
    own0 = gating(meta, 0, 4 * CAP)
    own1 = gating(meta, 1, 4 * CAP)

    def middle(j):
        first(1, j)
        second(0, j, theirs0)

    loop(middle)

    def late(j):
        third(0, j, own0)
        second(1, j, theirs1)

    loop(late)
    loop(lambda j: third(1, j, own1))

    meta_move.wait_send()
    for move in w_moves:
        move.wait_send()
    for f in range(2):
        for i in range(7):
            dispatch(f, i).wait_send()

        def drain(j):
            for i in range(5):
                combine(f, j, i).wait_send()
            handoff(f, j).wait()

        loop(drain)


def local(tokens, route_ids, slot_index, gate_values, w_gate, w_up, w_down):
    code = (route_ids[:, 0] * (CAP + 1) + slot_index[:, 0]).astype(F32)
    columns = jnp.concatenate([code, gate_values[:, 0]], axis=-1)
    columns = jnp.pad(columns, ((0, 0), (0, 0), (0, 128 - 4)))
    rows = jnp.pad(jnp.swapaxes(code, 1, 2), ((0, 0), (0, 6), (0, 128 - TOK)))
    meta = jnp.concatenate([columns, rows], axis=1)

    hbm = pl.BlockSpec(memory_space=pltpu.HBM)
    vmem = pl.BlockSpec(memory_space=pltpu.VMEM)
    dma = pltpu.SemaphoreType.DMA
    V = pltpu.VMEM
    shapes = ((2, TOK, D), (D, H), (D, H), (H, D))
    out = pl.pallas_call(
        kernel,
        out_shape=[jax.ShapeDtypeStruct(shape, BF) for shape in shapes],
        in_specs=[hbm, vmem, hbm, hbm, hbm],
        out_specs=[hbm] * 4,
        scratch_shapes=[
            V((2, TOK, D), BF), V((2, TOK, D), BF), V((2, TOK, D), BF), V((2, TOK + 8, 128), F32),
            V((2, 8 * CAP, D), BF), V((2, 2 * CAP, D), BF), V((2, 2 * CAP, D), BF), V((2, CAP, D), BF),
            V((2, 2, D, HC), BF), V((2, 2 * H, CW), BF), V((2, 8 * CAP, 2 * H), BF),
            V((2, NC, 2 * CAP, CW), BF), V((2, NC, 2 * CAP, CW), BF), V((2, NC, 2 * CAP, CW), BF),
            V((2, NC, CAP, CW), BF), V((2, NC, CAP, CW), BF), V((2, NC, CAP, CW), BF), V((2, NC, TOK, CW), BF),
            V((2, NC, 2 * CAP, CW), BF), V((2, NC, 2 * CAP, CW), BF),
            V((2, NC, CAP, CW), BF), V((2, NC, CAP, CW), BF), V((2, NC, TOK, CW), BF), V((2, NC, TOK, CW), BF),
            dma((2,)), dma((2, 2)), dma((2, 2)), dma((3,)), dma((3,)), dma, dma,
            dma((2, 7)), dma((2, 7)), dma((2, NC, 5)), dma((2, NC, 5)), dma((2, NC)), dma((2, NC)),
        ],
        compiler_params=pltpu.CompilerParams(
            collective_id=0, has_side_effects=True, vmem_limit_bytes=62 * 2**20
        ),
        name="relay_layer",
    )(tokens[:, 0], meta, w_gate[0, 0], w_up[0, 0], w_down[0, 0])
    return out[0][:, None]


def solution(mesh):
    spread = P(None, "section", "expert", None)
    split = P("section", "expert", None, None)
    return jax.shard_map(
        local,
        mesh=mesh,
        in_specs=(spread,) * 4 + (split,) * 3,
        out_specs=spread,
        check_vma=False,
    )
```

time: 603 us -> 173 us (0.29); the launches traced: 595 us -> 171 us
  waiting for transfers between devices: 420 us -> 0 us
  Pallas kernels: 0 us -> 166 us
  local copies, waits for them, and re-layouts: 67.1 us -> 2.95 us
  matrix products: 46.1 us -> 0 us
  starting transfers between devices: 33.3 us -> 0 us
  other arithmetic: 28.6 us -> 2.04 us
    all_to_all x3 -> x0, waiting for transfers between devices: 400 us -> none  [the longest x1 220 us: local(): lax.all_to_all(arrived, 'expert', split_axis=1, concat_axis=1, tiled=True)]
    pallas_call x0 -> x1, Pallas kernels: none -> 166 us  [local(): pl.pallas_call(kernel, out_shape=[jax.ShapeDtypeStruct(shape, BF) for sha...]
    dot_general x8 -> x0, matrix products: 46.1 us -> none  [the longest x1 10.3 us: expert_rows(): up = jnp.dot(rows, weight_up, preferred_element_type=jnp.float32)]
    mul x2 -> x0, local copies, waits for them, and re-layouts: 40.6 us -> none  [expert_rows(): coded_in.astype(jnp.float32).reshape(shape[:-1] + (D // TILE, TILE))]
    all_to_all x3 -> x0, starting transfers between devices: 29.1 us -> none  [the longest x1 13.7 us: local(): lax.all_to_all(arrived, 'expert', split_axis=1, concat_axis=1, tiled=True)]
    ppermute x2 -> x0, waiting for transfers between devices: 19.9 us -> none  [shifted(): return lax.ppermute(block, axis, route)]
    convert_element_type x1, other arithmetic: 15.4 us -> 0.7 us  [local(): code = (route_ids[:, 0] * (CAP + 1) + slot_index[:, 0]).astype(F32)]
    reduce_sum x1 -> x0, other arithmetic: 8.83 us -> none  [local(): jnp.sum(returned.astype(jnp.float32).reshape(2, nexp, WSPLIT, slots_cap,...]
  transfers between devices with their start and end apart: 5 -> 0, of which waited for: 3 -> 0; matrix products, arithmetic and copies ran while one was open for 10% -> 0% of each run, Pallas kernels for 0% -> 0%
where the time goes in v1:
time: 173 us; the launch traced here: 171 us
  Pallas kernels  166 us (96%)
  local copies, waits for them, and re-layouts  2.95 us (2%)
  other arithmetic  2.04 us (1%)
    pallas_call x1, Pallas kernels, local(): pl.pallas_call(kernel, out_shape=[jax.ShapeDtypeStruct(shape, BF) for sha...  166 us

profile of v1, /device:TPU:0, one launch (start us, length us, event | category | flops | bytes accessed | tf_op | source)
XLA Modules:
  0.0 171.4 jit_solution(2018521432439330606)
XLA Ops:
  0.0 0.7 fusion.2
  0.7 0.7 pad_maximum_fusion
  1.4 0.1 copy.12
  1.5 0.6 select_maximum_fusion.meta
  2.1 166.4 %relay_layer.1 = (bf16[2,64,7168]{2,1,0:T(8,128)(2,1)}, bf16[7168,512]{1,0:T(8,128)(2,1)}, bf16[7168,512]{1,0:T(8,128)(2,1)}, bf16[512,7168]{1,0:T(8,128)(2,1)}) custom-call(bf16[2,64,7168]{2,1,0:T(8,128)(2,1)} %bitcast.33, f32[2,72,128]{2,1,0:T(8,128)} %select_maximum_fusion.meta, bf16[7168,512]{1,0:T(8,128)(2,1)} %bitcast.29, bf16[7168,512]{1,0:T(8,128)(2,1)} %bitcast.30, ...), custom_call_target="tpu_custom_call" | custom-call | tf_op jit(solution)/shard_map/relay_layer/pallas_call | solution.py:328
  168.5 2.8 %copy.14 = bf16[2,1,64,7168]{3,2,1,0:T(8,128)(2,1)} copy(bf16[2,1,64,7168]{3,2,1,0:T(8,128)(2,1)} %bitcast.32) | data formatting | bytes 3670016

commit v2 on v0

v2 whole, which is shorter than its diff:
```python
import jax
import jax.numpy as jnp
from jax import lax
from jax.experimental import pallas as pl
from jax.experimental.pallas import tpu as pltpu
from jax.sharding import PartitionSpec as P

D = 7168
TILE = 128
TOK = 64
CAP = 32
H = 512
CW = 1024
NC = D // CW
STEPS = 2 * NC
HC = 256
KC = 1024
LAG = 2
ROW = 4
MESH = pl.DeviceIdType.MESH

CORE = 1
PAIR = 2
CROSS = 6
FAR = 8
DIAG = 14

BF = jnp.bfloat16
F32 = jnp.float32


def coarse(mag):
    lifted = mag * (2.0**20 + 1.0)
    return lifted - (lifted - mag)


def snap(values):
    mag = jnp.abs(values)
    near = coarse(mag)
    mirror = 2.0 * mag - near
    other = coarse(mirror)
    snapped = jnp.where(other == mirror, jnp.maximum(near, other), near)
    fine = jnp.floor(mag * 512.0 + 0.5) * (1.0 / 512.0)
    snapped = jnp.minimum(jnp.where(mag < 2.0**-6, fine, snapped), 448.0)
    return jnp.where(values < 0, -snapped, snapped)


def kernel(
    tok_hbm, ids, slots, gate_in, wg, wu, wd, out, wg2, wu2, wd2,
    tokv, rest, rest_p, meta, meta_p, gates,
    xrows, s_x, s_y, s_d,
    wbuf, dbuf, hid,
    loc, g_x, g_y, g_p, keep, g_d, g_t,
    r_x, r_y, r_p, r_d, r_t, fin,
    tok_sem, w_sem, d_sem, wx_s, wx_r, meta_s, meta_r,
    dis_s, dis_r, com_s, com_r,
):
    me = lax.axis_index("expert")
    sec = lax.axis_index("section")
    n_sec = lax.axis_size("section")
    up = lax.rem(sec + 1, n_sec)
    down = lax.rem(sec + n_sec - 1, n_sec)
    mine = (me // 8) * 2 + (me // 4) % 2

    flip = (lax.rem(sec, ROW) == 0).astype(jnp.int32)
    ends = (flip == 1) | (lax.rem(sec, ROW) == ROW - 1)

    def summed(f):
        return ends & (f == 1 - flip)

    def remote(src, dst, ss, rs, mask, section=sec):
        return pltpu.make_async_remote_copy(
            src_ref=src, dst_ref=dst, send_sem=ss, recv_sem=rs,
            device_id=(section, me ^ mask), device_id_type=MESH,
        )

    def columns(j):
        return pl.ds(pl.multiple_of(j * CW, CW), CW)

    def each(count, body):
        def step(j, carry):
            body(j)
            return carry

        lax.fori_loop(0, count, step, 0)

    def tok_copy(f):
        return pltpu.make_async_copy(tok_hbm.at[f], tokv.at[f], tok_sem.at[f])

    def w_copies(piece):
        gate_src, up_src = ((wg, wu), (wg2, wu2))[piece % 4 // 2]
        cols = pl.ds((piece % 2) * HC, HC)
        slot = piece % 2
        return (
            pltpu.make_async_copy(gate_src.at[:, cols], wbuf.at[slot, 0], w_sem.at[slot, 0]),
            pltpu.make_async_copy(up_src.at[:, cols], wbuf.at[slot, 1], w_sem.at[slot, 1]),
        )

    def d_copies(m):
        slot = lax.rem(m, 2)
        cols = columns(lax.rem(m, NC))
        return (
            pltpu.make_async_copy(wd.at[:, cols], dbuf.at[slot, pl.ds(0, H)], d_sem.at[slot, 0]),
            pltpu.make_async_copy(wd2.at[:, cols], dbuf.at[slot, pl.ds(H, H)], d_sem.at[slot, 1]),
        )

    for f in range(2):
        tok_copy(f).start()
    for cp in w_copies(0):
        cp.start()

    barrier = pltpu.get_barrier_semaphore()
    peers = [(sec, mask) for mask in (CORE, PAIR, CROSS, FAR, DIAG)]
    peers += [(up, 0), (down, 0)]
    for section, mask in peers:
        pl.semaphore_signal(barrier, inc=1, device_id=(section, me ^ mask), device_id_type=MESH)
    pl.semaphore_wait(barrier, len(peers))

    w_moves = [
        remote(src, dst, wx_s.at[i], wx_r.at[i], CORE)
        for i, (src, dst) in enumerate(((wg, wg2), (wu, wu2), (wd, wd2)))
    ]
    meta_move = remote(meta, meta_p, meta_s, meta_r, PAIR)

    def restore(f, j):
        for k in range(CW // TILE):
            cols = pl.ds(pl.multiple_of(j * CW, CW) + k * TILE, TILE)
            t = tokv[f, :, cols].astype(F32)
            scale = (jnp.max(jnp.abs(t), axis=-1, keepdims=True) + 1e-6) / 448.0
            rest[f, :, cols] = (snap(t * (1.0 / scale)) * scale).astype(BF)

    def selection(table, f, rows):
        row = lax.broadcasted_iota(jnp.int32, (rows, TOK), 0)
        code = ((mine ^ (row // CAP)) * (CAP + 1) + row % CAP).astype(F32)
        hit = (table[f, 0:1, :TOK] == code) | (table[f, 1:2, :TOK] == code)
        return jnp.where(hit, 1.0, 0.0).astype(BF)

    def gating(table, f):
        row = lax.broadcasted_iota(jnp.int32, (4 * CAP, 2 * TOK), 0)
        code = ((mine ^ (row // CAP)) * (CAP + 1) + row % CAP).astype(F32)
        weight = jnp.where(table[f, 0:1] == code, table[f, 2:3], 0.0)
        weight = weight + jnp.where(table[f, 1:2] == code, table[f, 3:4], 0.0)
        weight = weight.T[:TOK]
        high = weight.astype(BF)
        return high, (weight - high.astype(F32)).astype(BF)

    def pick(f, j, table, source, targets):
        sel = selection(table, f, len(targets) * CAP)
        cols = columns(j)
        got = jnp.dot(sel, source[f, :, cols], preferred_element_type=F32).astype(BF)
        for i, (ref, row) in enumerate(targets):
            ref[f, row : row + CAP, cols] = got[i * CAP : (i + 1) * CAP]

    def dispatch(f, j, i):
        cols = columns(j)

        def block(ref, b):
            return ref.at[f, pl.ds(b * CAP, CAP), cols]

        src, dst, mask = (
            lambda: (rest.at[f, :, cols], rest_p.at[f, :, cols], PAIR),
            lambda: (block(s_d, 0), block(xrows, 6), DIAG),
            lambda: (block(s_y, 0), block(xrows, 4), FAR),
            lambda: (block(s_x, 0), block(xrows, 2), CROSS),
            lambda: (block(s_y, 1), block(xrows, 5), FAR),
            lambda: (block(s_x, 1), block(xrows, 3), CROSS),
            lambda: (block(xrows, 6), block(xrows, 7), PAIR),
        )[i]()
        return remote(src, dst, dis_s.at[f, j, i], dis_r.at[f, j, i], mask)

    def send_own(f, j):
        restore(f, j)
        dispatch(f, j, 0).start()
        pick(f, j, meta, rest, ((xrows, 0), (s_x, 0), (s_y, 0), (s_d, 0)))
        for i in (1, 2, 3):
            dispatch(f, j, i).start()

    def send_partner(f, j):
        dispatch(f, j, 0).wait_recv()
        pick(f, j, meta_p, rest_p, ((xrows, CAP), (s_x, CAP), (s_y, CAP)))
        dispatch(f, j, 4).start()
        dispatch(f, j, 5).start()
        dispatch(f, j, 1).wait_recv()
        dispatch(f, j, 6).start()

    def rows_arrived(f):
        def body(j):
            for i in (2, 3, 4, 5, 6):
                dispatch(f, j, i).wait_recv()

        each(NC, body)

    def hidden(piece):
        turn, ci = divmod(piece, 4)
        f = jnp.where(flip == 1, 1 - turn, turn)
        if ci == 0:
            rows_arrived(f)
        for cp in w_copies(piece):
            cp.wait()
        if piece == 1:
            w_moves[0].wait_recv()
            w_moves[1].wait_recv()
        if piece < 7:
            for cp in w_copies(piece + 1):
                cp.start()

        def step(k, acc):
            rows = pl.ds(pl.multiple_of(k * KC, KC), KC)
            x = xrows[f, :, rows]
            g = jnp.dot(x, wbuf[piece % 2, 0, rows, :], preferred_element_type=F32)
            u = jnp.dot(x, wbuf[piece % 2, 1, rows, :], preferred_element_type=F32)
            return acc[0] + g, acc[1] + u

        zero = jnp.zeros((8 * CAP, HC), F32)
        g, u = lax.fori_loop(0, D // KC, step, (zero, zero))
        hid[f, :, ci * HC : (ci + 1) * HC] = (g / (1.0 + jnp.exp(-g)) * u).astype(BF)

    def combine(f, j, i):
        src, dst, mask = (
            lambda: (g_p.at[f, j, pl.ds(0, CAP)], r_p.at[f, j, pl.ds(0, CAP)], PAIR),
            lambda: (g_x.at[f, j], r_x.at[f, j], CROSS),
            lambda: (g_y.at[f, j], r_y.at[f, j], FAR),
            lambda: (g_t.at[f, j], r_t.at[f, j], PAIR),
            lambda: (g_d.at[f, j], r_d.at[f, j], DIAG),
            lambda: (g_p.at[f, j], r_p.at[f, j], PAIR),
            lambda: (g_y.at[f, j, pl.ds(0, CAP)], r_y.at[f, j, pl.ds(0, CAP)], FAR),
        )[i]()
        return remote(src, dst, com_s.at[f, j, i], com_r.at[f, j, i], mask)

    def handoff(f, j):
        section = jnp.where(f == 0, up, down)
        return remote(fin.at[f, j], out.at[f, :, columns(j)], com_s.at[f, j, 7], com_r.at[f, j, 7], 0, section)

    def gated(f, kind, cols, parts):
        z = jnp.concatenate(parts, axis=0)
        high = jnp.dot(gates[f, kind, 0, :, cols], z, preferred_element_type=F32)
        return high + jnp.dot(gates[f, kind, 1, :, cols], z, preferred_element_type=F32)

    def first(m, f, j):
        for cp in d_copies(m):
            cp.wait()

        @pl.when(m < STEPS - 1)
        def _():
            for cp in d_copies(m + 1):
                cp.start()

        q = jnp.dot(hid[f], dbuf[lax.rem(m, 2)], preferred_element_type=F32).astype(BF)
        g_p[f, j, :CAP] = q[7 * CAP :]
        g_p[f, j, CAP:] = q[5 * CAP : 6 * CAP]
        g_x[f, j] = q[2 * CAP : 4 * CAP]
        keep[f, j] = q[6 * CAP : 7 * CAP]
        g_y[f, j] = q[4 * CAP : 6 * CAP]
        combine(f, j, 1).start()

        @pl.when(summed(f))
        def _():
            combine(f, j, 5).start()

        @pl.when(jnp.logical_not(summed(f)))
        def _():
            combine(f, j, 0).start()
            combine(f, j, 2).start()

        loc[f, j] = q[: 2 * CAP]

    def add(a, b):
        return (a.astype(F32) + b.astype(F32)).astype(BF)

    def second(f, j):
        @pl.when(summed(f))
        def _():
            combine(f, j, 5).wait_recv()
            g_d[f, j] = add(keep[f, j], r_p[f, j, :CAP])
            combine(f, j, 4).start()
            g_y[f, j, :CAP] = add(g_y[f, j, :CAP], r_p[f, j, CAP:])
            combine(f, j, 6).start()
            combine(f, j, 1).wait_recv()
            parts = [loc[f, j, CAP:], r_x[f, j, CAP:]]
            g_t[f, j] = gated(f, 0, slice(0, 2 * CAP), parts).astype(BF)

        @pl.when(jnp.logical_not(summed(f)))
        def _():
            combine(f, j, 0).wait_recv()
            g_d[f, j] = add(keep[f, j], r_p[f, j, :CAP])
            combine(f, j, 4).start()
            combine(f, j, 1).wait_recv()
            combine(f, j, 2).wait_recv()
            parts = [loc[f, j, CAP:], r_x[f, j, CAP:], r_y[f, j, CAP:]]
            g_t[f, j] = gated(f, 0, slice(0, 3 * CAP), parts).astype(BF)

        combine(f, j, 3).start()

    def third(f, j):
        @pl.when(summed(f))
        def _():
            combine(f, j, 6).wait_recv()

        combine(f, j, 4).wait_recv()
        combine(f, j, 3).wait_recv()
        parts = [loc[f, j, :CAP], r_x[f, j, :CAP], r_y[f, j, :CAP], r_d[f, j]]
        total = gated(f, 1, slice(0, 4 * CAP), parts)
        total = total + r_t[f, j].astype(F32) + tokv[f, :, columns(j)].astype(F32)
        fin[f, j] = total.astype(BF)
        handoff(f, j).start()

    def at(step, lag, body):
        n = step - lag

        @pl.when((n >= 0) & (n < STEPS))
        def _():
            turn = n // NC
            body(jnp.where(flip == 1, 1 - turn, turn), n - turn * NC)

    meta[...] = jnp.zeros_like(meta)
    for f in range(2):
        meta[f, 0:2, :TOK] = (ids[f] * (CAP + 1) + slots[f]).astype(F32)
        meta[f, 2:4, :TOK] = gate_in[f]
    meta_move.start()
    for f in range(2):
        tok_copy(f).wait()
    send_own(flip, 0)
    for move in w_moves:
        move.start()
    meta_move.wait_recv()

    def dispatch_step(n):
        @pl.when(n > 0)
        def _():
            at(n, 0, send_own)

        at(n, LAG, send_partner)
        for ci in range(4):

            @pl.when(n == NC + LAG + 1 + ci)
            def _():
                hidden(ci)

    each(STEPS + LAG, dispatch_step)

    w_moves[2].wait_recv()
    for cp in d_copies(0):
        cp.start()
    for f in range(2):
        for kind, table in enumerate((meta_p, meta)):
            gates[f, kind, 0], gates[f, kind, 1] = gating(table, f)

    def combine_step(m):
        at(m, 0, lambda f, j: first(m, f, j))
        for ci in range(4):

            @pl.when(m == 1 + ci)
            def _():
                hidden(4 + ci)

        at(m, LAG, second)
        at(m, 2 * LAG, third)

    each(STEPS + 2 * LAG, combine_step)

    for move in w_moves + [meta_move]:
        move.wait_send()

    def drain(n):
        f = n // NC
        j = n - f * NC
        for i in range(7):
            dispatch(f, j, i).wait_send()
        for i in (1, 3, 4):
            combine(f, j, i).wait_send()

        @pl.when(summed(f))
        def _():
            combine(f, j, 5).wait_send()
            combine(f, j, 6).wait_send()

        @pl.when(jnp.logical_not(summed(f)))
        def _():
            combine(f, j, 0).wait_send()
            combine(f, j, 2).wait_send()

        handoff(f, j).wait()

    each(STEPS, drain)


def local(tokens, route_ids, slot_index, gate_values, w_gate, w_up, w_down):
    routing = [jnp.swapaxes(x[:, 0], 1, 2) for x in (route_ids, slot_index, gate_values)]
    hbm = pl.BlockSpec(memory_space=pltpu.HBM)
    vmem = pl.BlockSpec(memory_space=pltpu.VMEM)
    dma = pltpu.SemaphoreType.DMA

    def buf(*shape):
        return pltpu.VMEM(shape, BF)

    table = pltpu.VMEM((2, 8, 2 * TOK), F32)
    half = buf(2, NC, CAP, CW)
    whole = buf(2, NC, TOK, CW)
    shapes = ((2, TOK, D), (D, H), (D, H), (H, D))
    out = pl.pallas_call(
        kernel,
        out_shape=[jax.ShapeDtypeStruct(shape, BF) for shape in shapes],
        in_specs=[hbm, vmem, vmem, vmem, hbm, hbm, hbm],
        out_specs=[hbm] * 4,
        scratch_shapes=[
            buf(2, TOK, D), buf(2, TOK, D), buf(2, TOK, D), table, table, buf(2, 2, 2, TOK, 4 * CAP),
            buf(2, 8 * CAP, D), buf(2, 2 * CAP, D), buf(2, 2 * CAP, D), buf(2, CAP, D),
            buf(2, 2, D, HC), buf(2, 2 * H, CW), buf(2, 8 * CAP, 2 * H),
            whole, whole, whole, whole, half, half, whole,
            whole, whole, whole, half, whole, whole,
            dma((2,)), dma((2, 2)), dma((2, 2)), dma((3,)), dma((3,)), dma, dma,
            dma((2, NC, 7)), dma((2, NC, 7)), dma((2, NC, 8)), dma((2, NC, 8)),
        ],
        compiler_params=pltpu.CompilerParams(
            collective_id=0, has_side_effects=True, vmem_limit_bytes=63 * 2**20
        ),
        name="relay_layer",
    )(tokens[:, 0], *routing, w_gate[0, 0], w_up[0, 0], w_down[0, 0])
    return out[0][:, None]


def solution(mesh):
    spread = P(None, "section", "expert", None)
    split = P("section", "expert", None, None)
    return jax.shard_map(
        local,
        mesh=mesh,
        in_specs=(spread,) * 4 + (split,) * 3,
        out_specs=spread,
        check_vma=False,
    )
```

time: 603 us -> 162 us (0.27)
  the two profiles are of different devices: /device:TPU:0 before, /device:TPU:4 now
where the time goes in v2:
time: 162 us; the launch traced here: 161 us
  Pallas kernels  159 us (98%)
  local copies, waits for them, and re-layouts  2.85 us (2%)
    pallas_call x1, Pallas kernels, local(): pl.pallas_call(kernel, out_shape=[jax.ShapeDtypeStruct(shape, BF) for sha...  159 us

profile of v2, /device:TPU:4, one launch (start us, length us, event | category | flops | bytes accessed | tf_op | source)
XLA Modules:
  0.0 161.5 jit_solution(18029636020119364163)
XLA Ops:
  0.0 158.6 %relay_layer.1 = (bf16[2,64,7168]{2,1,0:T(8,128)(2,1)}, bf16[7168,512]{1,0:T(8,128)(2,1)}, bf16[7168,512]{1,0:T(8,128)(2,1)}, bf16[512,7168]{1,0:T(8,128)(2,1)}) custom-call(bf16[2,64,7168]{2,1,0:T(8,128)(2,1)} %bitcast.20, s32[2,2,64]{2,1,0:T(2,128)} %bitcast.21, s32[2,2,64]{2,1,0:T(2,128)} %bitcast.22, f32[2,2,64]{2,1,0:T(2,128)} %bitcast.23, ...), custom_call_target="tpu_custom_call" | custom-call | tf_op jit(solution)/shard_map/relay_layer/pallas_call | solution.py:400
  158.6 2.8 %copy.10 = bf16[2,1,64,7168]{3,2,1,0:T(8,128)(2,1)} copy(bf16[2,1,64,7168]{3,2,1,0:T(8,128)(2,1)} %bitcast.19) | data formatting | bytes 3670016

commit v3 on v2

--- a/solution.py
+++ b/solution.py
@@ -13,9 +13,10 @@
 CW = 1024
 NC = D // CW
 STEPS = 2 * NC
-HC = 256
-KC = 1024
-LAG = 2
+LAG = 4
+SECOND = 4
+THIRD = 8
+LATE = 6
 ROW = 4
 MESH = pl.DeviceIdType.MESH
 
@@ -49,10 +50,10 @@
     tok_hbm, ids, slots, gate_in, wg, wu, wd, out, wg2, wu2, wd2,
     tokv, rest, rest_p, meta, meta_p, gates,
     xrows, s_x, s_y, s_d,
-    wbuf, dbuf, hid,
+    wbuf, dbuf, acc, hid,
     loc, g_x, g_y, g_p, keep, g_d, g_t,
     r_x, r_y, r_p, r_d, r_t, fin,
-    tok_sem, w_sem, d_sem, wx_s, wx_r, meta_s, meta_r,
+    tok_sem, w_sem, d_sem, wx_s, wx_r, dx_s, dx_r, meta_s, meta_r,
     dis_s, dis_r, com_s, com_r,
 ):
     me = lax.axis_index("expert")
@@ -87,14 +88,13 @@
     def tok_copy(f):
         return pltpu.make_async_copy(tok_hbm.at[f], tokv.at[f], tok_sem.at[f])
 
-    def w_copies(piece):
-        gate_src, up_src = ((wg, wu), (wg2, wu2))[piece % 4 // 2]
-        cols = pl.ds((piece % 2) * HC, HC)
-        slot = piece % 2
-        return (
-            pltpu.make_async_copy(gate_src.at[:, cols], wbuf.at[slot, 0], w_sem.at[slot, 0]),
-            pltpu.make_async_copy(up_src.at[:, cols], wbuf.at[slot, 1], w_sem.at[slot, 1]),
-        )
+    def w_copies(k):
+        slot = lax.rem(k, 2)
+        rows = columns(lax.rem(k, NC))
+        return [
+            pltpu.make_async_copy(src.at[rows], wbuf.at[slot, i], w_sem.at[slot, i])
+            for i, src in enumerate((wg, wu, wg2, wu2))
+        ]
 
     def d_copies(m):
         slot = lax.rem(m, 2)
@@ -106,8 +106,6 @@
 
     for f in range(2):
         tok_copy(f).start()
-    for cp in w_copies(0):
-        cp.start()
 
     barrier = pltpu.get_barrier_semaphore()
     peers = [(sec, mask) for mask in (CORE, PAIR, CROSS, FAR, DIAG)]
@@ -116,10 +114,12 @@
         pl.semaphore_signal(barrier, inc=1, device_id=(section, me ^ mask), device_id_type=MESH)
     pl.semaphore_wait(barrier, len(peers))
 
-    w_moves = [
-        remote(src, dst, wx_s.at[i], wx_r.at[i], CORE)
-        for i, (src, dst) in enumerate(((wg, wg2), (wu, wu2), (wd, wd2)))
-    ]
+    def w_move(i, j):
+        src, dst = ((wg, wg2), (wu, wu2))[i]
+        rows = columns(j)
+        return remote(src.at[rows], dst.at[rows], wx_s.at[j, i], wx_r.at[j, i], CORE)
+
+    d_move = remote(wd, wd2, dx_s, dx_r, CORE)
     meta_move = remote(meta, meta_p, meta_s, meta_r, PAIR)
 
     def restore(f, j):
@@ -183,37 +183,38 @@
         dispatch(f, j, 1).wait_recv()
         dispatch(f, j, 6).start()
 
-    def rows_arrived(f):
-        def body(j):
-            for i in (2, 3, 4, 5, 6):
-                dispatch(f, j, i).wait_recv()
-
-        each(NC, body)
-
-    def hidden(piece):
-        turn, ci = divmod(piece, 4)
-        f = jnp.where(flip == 1, 1 - turn, turn)
-        if ci == 0:
-            rows_arrived(f)
-        for cp in w_copies(piece):
+    def load_weights(k):
+        @pl.when(k < NC)
+        def _():
+            w_move(0, k).wait_recv()
+            w_move(1, k).wait_recv()
+
+        for cp in w_copies(k):
+            cp.start()
+
+    def hidden(k, f, j):
+        for i in (2, 3, 4, 5, 6):
+            dispatch(f, j, i).wait_recv()
+        for cp in w_copies(k):
             cp.wait()
-        if piece == 1:
-            w_moves[0].wait_recv()
-            w_moves[1].wait_recv()
-        if piece < 7:
-            for cp in w_copies(piece + 1):
-                cp.start()
-
-        def step(k, acc):
-            rows = pl.ds(pl.multiple_of(k * KC, KC), KC)
-            x = xrows[f, :, rows]
-            g = jnp.dot(x, wbuf[piece % 2, 0, rows, :], preferred_element_type=F32)
-            u = jnp.dot(x, wbuf[piece % 2, 1, rows, :], preferred_element_type=F32)
-            return acc[0] + g, acc[1] + u
-
-        zero = jnp.zeros((8 * CAP, HC), F32)
-        g, u = lax.fori_loop(0, D // KC, step, (zero, zero))
-        hid[f, :, ci * HC : (ci + 1) * HC] = (g / (1.0 + jnp.exp(-g)) * u).astype(BF)
+
+        @pl.when(k < STEPS - 1)
+        def _():
+            load_weights(k + 1)
+
+        @pl.when(j == 0)
+        def _():
+            acc[...] = jnp.zeros_like(acc)
+
+        x = xrows[f, :, columns(j)]
+        for i in range(4):
+            acc[i] += jnp.dot(x, wbuf[lax.rem(k, 2), i], preferred_element_type=F32)
+
+        @pl.when(j == NC - 1)
+        def _():
+            for i in range(2):
+                g = acc[2 * i]
+                hid[f, :, i * H : (i + 1) * H] = (g / (1.0 + jnp.exp(-g)) * acc[2 * i + 1]).astype(BF)
 
     def combine(f, j, i):
         src, dst, mask = (
@@ -320,46 +321,47 @@
     for f in range(2):
         tok_copy(f).wait()
     send_own(flip, 0)
-    for move in w_moves:
-        move.start()
+    for j in range(NC):
+        w_move(0, j).start()
+        w_move(1, j).start()
+    d_move.start()
     meta_move.wait_recv()
-
-    def dispatch_step(n):
-        @pl.when(n > 0)
-        def _():
-            at(n, 0, send_own)
-
-        at(n, LAG, send_partner)
-        for ci in range(4):
-
-            @pl.when(n == NC + LAG + 1 + ci)
-            def _():
-                hidden(ci)
-
-    each(STEPS + LAG, dispatch_step)
-
-    w_moves[2].wait_recv()
-    for cp in d_copies(0):
-        cp.start()
     for f in range(2):
         for kind, table in enumerate((meta_p, meta)):
             gates[f, kind, 0], gates[f, kind, 1] = gating(table, f)
 
-    def combine_step(m):
-        at(m, 0, lambda f, j: first(m, f, j))
-        for ci in range(4):
-
-            @pl.when(m == 1 + ci)
-            def _():
-                hidden(4 + ci)
-
-        at(m, LAG, second)
-        at(m, 2 * LAG, third)
-
-    each(STEPS + 2 * LAG, combine_step)
-
-    for move in w_moves + [meta_move]:
-        move.wait_send()
+    def step(n):
+        @pl.when(n > 0)
+        def _():
+            at(n, 0, send_own)
+
+        at(n, LAG, send_partner)
+
+        @pl.when(n == LATE - 1)
+        def _():
+            load_weights(0)
+
+        @pl.when(n == STEPS - 1)
+        def _():
+            d_move.wait_recv()
+            for cp in d_copies(0):
+                cp.start()
+
+        at(n, STEPS, lambda f, j: first(n - STEPS, f, j))
+        at(n, STEPS + SECOND, second)
+        at(n, STEPS + THIRD, third)
+        at(n, LATE, lambda f, j: hidden(n - LATE, f, j))
+
+    each(2 * STEPS + THIRD, step)
+
+    meta_move.wait_send()
+    d_move.wait_send()
+
+    def drain_weights(j):
+        w_move(0, j).wait_send()
+        w_move(1, j).wait_send()
+
+    each(NC, drain_weights)
 
     def drain(n):
         f = n // NC
@@ -405,10 +407,10 @@
         scratch_shapes=[
             buf(2, TOK, D), buf(2, TOK, D), buf(2, TOK, D), table, table, buf(2, 2, 2, TOK, 4 * CAP),
             buf(2, 8 * CAP, D), buf(2, 2 * CAP, D), buf(2, 2 * CAP, D), buf(2, CAP, D),
-            buf(2, 2, D, HC), buf(2, 2 * H, CW), buf(2, 8 * CAP, 2 * H),
+            buf(2, 4, CW, H), buf(2, 2 * H, CW), pltpu.VMEM((4, 8 * CAP, H), F32), buf(2, 8 * CAP, 2 * H),
             whole, whole, whole, whole, half, half, whole,
             whole, whole, whole, half, whole, whole,
-            dma((2,)), dma((2, 2)), dma((2, 2)), dma((3,)), dma((3,)), dma, dma,
+            dma((2,)), dma((2, 4)), dma((2, 2)), dma((NC, 2)), dma((NC, 2)), dma, dma, dma, dma,
             dma((2, NC, 7)), dma((2, NC, 7)), dma((2, NC, 8)), dma((2, NC, 8)),
         ],
         compiler_params=pltpu.CompilerParams(

time: 162 us -> 150 us (0.926)
  the two profiles are of different devices: /device:TPU:4 before, /device:TPU:0 now
where the time goes in v3:
time: 150 us; the launch traced here: 149 us
  Pallas kernels  146 us (97%)
  local copies, waits for them, and re-layouts  2.85 us (2%)
    pallas_call x1, Pallas kernels, local(): pl.pallas_call(kernel, out_shape=[jax.ShapeDtypeStruct(shape, BF) for sha...  146 us

profile of v3, /device:TPU:0, one launch (start us, length us, event | category | flops | bytes accessed | tf_op | source)
XLA Modules:
  0.0 149.0 jit_solution(8143656877462746555)
XLA Ops:
  0.0 146.2 %relay_layer.1 = (bf16[2,64,7168]{2,1,0:T(8,128)(2,1)}, bf16[7168,512]{1,0:T(8,128)(2,1)}, bf16[7168,512]{1,0:T(8,128)(2,1)}, bf16[512,7168]{1,0:T(8,128)(2,1)}) custom-call(bf16[2,64,7168]{2,1,0:T(8,128)(2,1)} %bitcast.20, s32[2,2,64]{2,1,0:T(2,128)} %bitcast.21, s32[2,2,64]{2,1,0:T(2,128)} %bitcast.22, f32[2,2,64]{2,1,0:T(2,128)} %bitcast.23, ...), custom_call_target="tpu_custom_call" | custom-call | tf_op jit(solution)/shard_map/relay_layer/pallas_call | solution.py:402
  146.2 2.8 %copy.10 = bf16[2,1,64,7168]{3,2,1,0:T(8,128)(2,1)} copy(bf16[2,1,64,7168]{3,2,1,0:T(8,128)(2,1)} %bitcast.19) | data formatting | bytes 3670016

commit v4 on v3

--- a/solution.py
+++ b/solution.py
@@ -16,6 +16,8 @@
 LAG = 4
 SECOND = 4
 THIRD = 8
+RELAY = 10
+SUMMED = 5
 LATE = 6
 ROW = 4
 MESH = pl.DeviceIdType.MESH
@@ -52,9 +54,9 @@
     xrows, s_x, s_y, s_d,
     wbuf, dbuf, acc, hid,
     loc, g_x, g_y, g_p, keep, g_d, g_t,
-    r_x, r_y, r_p, r_d, r_t, fin,
+    r_x, r_y, r_p, r_d, r_t, fin, half_way,
     tok_sem, w_sem, d_sem, wx_s, wx_r, dx_s, dx_r, meta_s, meta_r,
-    dis_s, dis_r, com_s, com_r,
+    dis_s, dis_r, com_s, com_r, way_s, way_r, last_r,
 ):
     me = lax.axis_index("expert")
     sec = lax.axis_index("section")
@@ -65,9 +67,17 @@
 
     flip = (lax.rem(sec, ROW) == 0).astype(jnp.int32)
     ends = (flip == 1) | (lax.rem(sec, ROW) == ROW - 1)
-
-    def summed(f):
+    to_relay = sec ^ (ROW + 1)
+    from_relay = sec ^ 2
+
+    def wraps(f):
+        return ends & (f == flip)
+
+    def arrives(f):
         return ends & (f == 1 - flip)
+
+    def summed(f, j):
+        return (f == 1 - flip) & (j < SUMMED)
 
     def remote(src, dst, ss, rs, mask, section=sec):
         return pltpu.make_async_remote_copy(
@@ -109,7 +119,7 @@
 
     barrier = pltpu.get_barrier_semaphore()
     peers = [(sec, mask) for mask in (CORE, PAIR, CROSS, FAR, DIAG)]
-    peers += [(up, 0), (down, 0)]
+    peers += [(up, 0), (down, 0), (to_relay, 0), (from_relay, 0)]
     for section, mask in peers:
         pl.semaphore_signal(barrier, inc=1, device_id=(section, me ^ mask), device_id_type=MESH)
     pl.semaphore_wait(barrier, len(peers))
@@ -232,6 +242,33 @@
         section = jnp.where(f == 0, up, down)
         return remote(fin.at[f, j], out.at[f, :, columns(j)], com_s.at[f, j, 7], com_r.at[f, j, 7], 0, section)
 
+    def first_half(f, j):
+        section = jnp.where(f == 0, up, down)
+        rows = pl.ds(0, CAP)
+        return remote(fin.at[f, j, rows], out.at[f, rows, columns(j)], com_s.at[f, j, 7], com_r.at[f, j, 7], 0, section)
+
+    def second_half(f, j):
+        return remote(fin.at[f, j, pl.ds(CAP, CAP)], half_way.at[j], way_s.at[j], way_r.at[j], 0, to_relay)
+
+    def relayed(f, j):
+        return remote(half_way.at[j], out.at[f, pl.ds(CAP, CAP), columns(j)], way_s.at[j], last_r.at[j], 0, from_relay)
+
+    def hand_over(f, j):
+        @pl.when(wraps(f))
+        def _():
+            first_half(f, j).start()
+            second_half(f, j).start()
+
+        @pl.when(jnp.logical_not(wraps(f)))
+        def _():
+            handoff(f, j).start()
+
+    front_between = (lax.rem(sec, ROW) == 1).astype(jnp.int32)
+
+    def relay(j):
+        second_half(front_between, j).wait_recv()
+        relayed(front_between, j).start()
+
     def gated(f, kind, cols, parts):
         z = jnp.concatenate(parts, axis=0)
         high = jnp.dot(gates[f, kind, 0, :, cols], z, preferred_element_type=F32)
@@ -254,11 +291,11 @@
         g_y[f, j] = q[4 * CAP : 6 * CAP]
         combine(f, j, 1).start()
 
-        @pl.when(summed(f))
+        @pl.when(summed(f, j))
         def _():
             combine(f, j, 5).start()
 
-        @pl.when(jnp.logical_not(summed(f)))
+        @pl.when(jnp.logical_not(summed(f, j)))
         def _():
             combine(f, j, 0).start()
             combine(f, j, 2).start()
@@ -269,7 +306,7 @@
         return (a.astype(F32) + b.astype(F32)).astype(BF)
 
     def second(f, j):
-        @pl.when(summed(f))
+        @pl.when(summed(f, j))
         def _():
             combine(f, j, 5).wait_recv()
             g_d[f, j] = add(keep[f, j], r_p[f, j, :CAP])
@@ -280,7 +317,7 @@
             parts = [loc[f, j, CAP:], r_x[f, j, CAP:]]
             g_t[f, j] = gated(f, 0, slice(0, 2 * CAP), parts).astype(BF)
 
-        @pl.when(jnp.logical_not(summed(f)))
+        @pl.when(jnp.logical_not(summed(f, j)))
         def _():
             combine(f, j, 0).wait_recv()
             g_d[f, j] = add(keep[f, j], r_p[f, j, :CAP])
@@ -293,7 +330,7 @@
         combine(f, j, 3).start()
 
     def third(f, j):
-        @pl.when(summed(f))
+        @pl.when(summed(f, j))
         def _():
             combine(f, j, 6).wait_recv()
 
@@ -303,7 +340,7 @@
         total = gated(f, 1, slice(0, 4 * CAP), parts)
         total = total + r_t[f, j].astype(F32) + tokv[f, :, columns(j)].astype(F32)
         fin[f, j] = total.astype(BF)
-        handoff(f, j).start()
+        hand_over(f, j)
 
     def at(step, lag, body):
         n = step - lag
@@ -352,6 +389,11 @@
         at(n, STEPS + THIRD, third)
         at(n, LATE, lambda f, j: hidden(n - LATE, f, j))
 
+        @pl.when(jnp.logical_not(ends) & (n >= STEPS + RELAY) & (n < STEPS + RELAY + NC))
+        def _():
+            relay(n - STEPS - RELAY)
+
+
     each(2 * STEPS + THIRD, step)
 
     meta_move.wait_send()
@@ -371,19 +413,40 @@
         for i in (1, 3, 4):
             combine(f, j, i).wait_send()
 
-        @pl.when(summed(f))
+        @pl.when(summed(f, j))
         def _():
             combine(f, j, 5).wait_send()
             combine(f, j, 6).wait_send()
 
-        @pl.when(jnp.logical_not(summed(f)))
+        @pl.when(jnp.logical_not(summed(f, j)))
         def _():
             combine(f, j, 0).wait_send()
             combine(f, j, 2).wait_send()
 
-        handoff(f, j).wait()
+        @pl.when(wraps(f))
+        def _():
+            first_half(f, j).wait_send()
+            second_half(f, j).wait_send()
+
+        @pl.when(jnp.logical_not(wraps(f)))
+        def _():
+            handoff(f, j).wait_send()
+
+        @pl.when(arrives(f))
+        def _():
+            first_half(f, j).wait_recv()
+            relayed(f, j).wait_recv()
+
+        @pl.when(jnp.logical_not(arrives(f)))
+        def _():
+            handoff(f, j).wait_recv()
+
 
     each(STEPS, drain)
+
+    @pl.when(jnp.logical_not(ends))
+    def _():
+        each(NC, lambda j: relayed(front_between, j).wait_send())
 
 
 def local(tokens, route_ids, slot_index, gate_values, w_gate, w_up, w_down):
@@ -409,9 +472,9 @@
             buf(2, 8 * CAP, D), buf(2, 2 * CAP, D), buf(2, 2 * CAP, D), buf(2, CAP, D),
             buf(2, 4, CW, H), buf(2, 2 * H, CW), pltpu.VMEM((4, 8 * CAP, H), F32), buf(2, 8 * CAP, 2 * H),
             whole, whole, whole, whole, half, half, whole,
-            whole, whole, whole, half, whole, whole,
+            whole, whole, whole, half, whole, whole, buf(NC, CAP, CW),
             dma((2,)), dma((2, 4)), dma((2, 2)), dma((NC, 2)), dma((NC, 2)), dma, dma, dma, dma,
-            dma((2, NC, 7)), dma((2, NC, 7)), dma((2, NC, 8)), dma((2, NC, 8)),
+            dma((2, NC, 7)), dma((2, NC, 7)), dma((2, NC, 8)), dma((2, NC, 8)), dma((NC,)), dma((NC,)), dma((NC,)),
         ],
         compiler_params=pltpu.CompilerParams(
             collective_id=0, has_side_effects=True, vmem_limit_bytes=63 * 2**20

time: 150 us -> 147 us (0.980)
  Pallas kernels: 146 us -> 144 us
    pallas_call x1, Pallas kernels: 146 us -> 144 us  [local(): pl.pallas_call(kernel, out_shape=[jax.ShapeDtypeStruct(shape, BF) for sha...]
where the time goes in v4:
time: 147 us
  Pallas kernels  144 us (98%)
  local copies, waits for them, and re-layouts  2.85 us (2%)
    pallas_call x1, Pallas kernels, local(): pl.pallas_call(kernel, out_shape=[jax.ShapeDtypeStruct(shape, BF) for sha...  144 us

profile of v4, /device:TPU:0, one launch (start us, length us, event | category | flops | bytes accessed | tf_op | source)
XLA Modules:
  0.0 146.8 jit_solution(2173332223275783123)
XLA Ops:
  0.0 143.9 %relay_layer.1 = (bf16[2,64,7168]{2,1,0:T(8,128)(2,1)}, bf16[7168,512]{1,0:T(8,128)(2,1)}, bf16[7168,512]{1,0:T(8,128)(2,1)}, bf16[512,7168]{1,0:T(8,128)(2,1)}) custom-call(bf16[2,64,7168]{2,1,0:T(8,128)(2,1)} %bitcast.20, s32[2,2,64]{2,1,0:T(2,128)} %bitcast.21, s32[2,2,64]{2,1,0:T(2,128)} %bitcast.22, f32[2,2,64]{2,1,0:T(2,128)} %bitcast.23, ...), custom_call_target="tpu_custom_call" | custom-call | tf_op jit(solution)/shard_map/relay_layer/pallas_call | solution.py:465
  143.9 2.8 %copy.10 = bf16[2,1,64,7168]{3,2,1,0:T(8,128)(2,1)} copy(bf16[2,1,64,7168]{3,2,1,0:T(8,128)(2,1)} %bitcast.19) | data formatting | bytes 3670016

commit v5 on v4

--- a/solution.py
+++ b/solution.py
@@ -15,8 +15,8 @@
 STEPS = 2 * NC
 LAG = 4
 SECOND = 4
-THIRD = 8
-RELAY = 10
+THIRD = 7
+RELAY = 9
 SUMMED = 5
 LATE = 6
 ROW = 4
@@ -289,8 +289,6 @@
         g_x[f, j] = q[2 * CAP : 4 * CAP]
         keep[f, j] = q[6 * CAP : 7 * CAP]
         g_y[f, j] = q[4 * CAP : 6 * CAP]
-        combine(f, j, 1).start()
-
         @pl.when(summed(f, j))
         def _():
             combine(f, j, 5).start()
@@ -300,6 +298,7 @@
             combine(f, j, 0).start()
             combine(f, j, 2).start()
 
+        combine(f, j, 1).start()
         loc[f, j] = q[: 2 * CAP]
 
     def add(a, b):

time: 147 us -> 147 us (level)
  no operation moved by 1% of the time
where the time goes in v5:
time: 147 us
  Pallas kernels  144 us (98%)
  local copies, waits for them, and re-layouts  2.85 us (2%)
    pallas_call x1, Pallas kernels, local(): pl.pallas_call(kernel, out_shape=[jax.ShapeDtypeStruct(shape, BF) for sha...  144 us

profile of v5, /device:TPU:0, one launch (start us, length us, event | category | flops | bytes accessed | tf_op | source)
XLA Modules:
  0.0 146.8 jit_solution(14970659571821231725)
XLA Ops:
  0.0 143.9 %relay_layer.1 = (bf16[2,64,7168]{2,1,0:T(8,128)(2,1)}, bf16[7168,512]{1,0:T(8,128)(2,1)}, bf16[7168,512]{1,0:T(8,128)(2,1)}, bf16[512,7168]{1,0:T(8,128)(2,1)}) custom-call(bf16[2,64,7168]{2,1,0:T(8,128)(2,1)} %bitcast.20, s32[2,2,64]{2,1,0:T(2,128)} %bitcast.21, s32[2,2,64]{2,1,0:T(2,128)} %bitcast.22, f32[2,2,64]{2,1,0:T(2,128)} %bitcast.23, ...), custom_call_target="tpu_custom_call" | custom-call | tf_op jit(solution)/shard_map/relay_layer/pallas_call | solution.py:464
  143.9 2.8 %copy.10 = bf16[2,1,64,7168]{3,2,1,0:T(8,128)(2,1)} copy(bf16[2,1,64,7168]{3,2,1,0:T(8,128)(2,1)} %bitcast.19) | data formatting | bytes 3670016
